TPU v7x, 32 devices: a whole 2x2x4 slice. The times are simulated.
32 devices in a mesh: groups: 2 (over y), tm: 4 (over z), chan: 2 (over x), dp: 2 (over core).
Axes of the slice: x: 2, y: 2, z: 4, core: 2. Of those that a mesh axis runs over, the one named last changes fastest.
Arguments:
- frames: bfloat16 [4, 32, 16, 16, 512], P(('groups', 'dp'), 'tm'), parts along dimension 0, may hold values from -6 to 6
- w_in: bfloat16 [3, 3, 512, 256], P(None, None, None, 'chan'), may hold values from -0.09375 to 0.09375
- w_out: bfloat16 [3, 3, 256, 512], P(None, None, None, 'chan'), may hold values from -0.01171875 to 0.01171875
- skip: float32 [512], P('chan'), may hold values from -4 to 4
- rates: float32 [256], replicated, may hold values from 0.002 to 0.3, as said below
- steps_dt: float32 [4, 32], P(('groups', 'dp'), 'tm'), parts along dimension 0, may hold values from 0.5 to 80, as said below
Outputs:
- mixed: bfloat16 [4, 32, 16, 16, 512], P(('groups', 'dp'), 'tm', None, None, 'chan'), parts along dimension 0
There are 2 independent parts, one for each index of `groups`. A program takes and returns all parts, laid end to end along the dimension named above; an argument that names none is the same for every part. Nothing has to cross between parts.
Inputs may be any that keep to these rules, and one draw needn't show every extreme that they name: rates are positive. `steps_dt`: time steps are positive.
All inputs are finite; a program needn't handle non-finite values.
Results may differ from a plain program's by a relative error of at most 0.0051.
Values may be sent and summed in bfloat16 or wider, within the bound.
A program may use at most 64 MiB of HBM per device.

v0:
```python
import jax
import jax.numpy as jnp
from jax import lax
from jax.sharding import PartitionSpec as P


def from_behind(block, axis, distance):
    devices = range(lax.axis_size(axis))
    route = [(i - distance, i) for i in devices if i - distance in devices]
    return lax.ppermute(block, axis, route)


def pad_grid(values):
    return jnp.pad(values, ((0, 0), (0, 0), (1, 1), (1, 1), (0, 0)))


def displaced_filter(padded, weight, total):
    height = padded.shape[2] - 2
    width = padded.shape[3] - 2
    channels = padded.shape[4]
    for row_off in range(3):
        for col_off in range(3):
            window = padded[:, :, row_off : row_off + height, col_off : col_off + width, :].reshape(
                -1, channels
            )
            term = jnp.dot(window, weight[row_off, col_off], preferred_element_type=jnp.float32)
            total = total + term.reshape(total.shape)
    return total


def combine_operator(earlier, later):
    return (earlier[0] * later[0], later[0] * earlier[1] + later[1])


def block_states(frames, weight_in, rate_part, steps_dt):
    batch_n, frame_n, height, width = frames.shape[:4]
    chans = weight_in.shape[3]
    shape_out = frames.shape[:4] + (chans,)
    drive = displaced_filter(pad_grid(frames), weight_in, jnp.zeros(shape_out, jnp.float32))
    flat_drive = drive.reshape(batch_n, frame_n, height, width * chans)
    scaled = rate_part[None, None, :] * steps_dt[:, :, None]
    decay = jnp.exp(-scaled)
    gain_in = -jnp.expm1(-scaled) / rate_part[None, None, :]
    decay_flat = jnp.tile(decay, (1, 1, width))[:, :, None, :]
    gain_flat = jnp.tile(gain_in, (1, 1, width))[:, :, None, :]
    running_product, local_state = lax.associative_scan(
        combine_operator, (decay_flat, gain_flat * flat_drive), axis=1
    )
    total_decay = running_product[:, -1]
    end_state = local_state[:, -1]

    def relay(index, incoming):
        return from_behind(total_decay * incoming + end_state, "tm", 1)

    carried = lax.fori_loop(0, lax.axis_size("tm") - 1, relay, jnp.zeros_like(end_state))
    full_state = local_state + running_product * carried[:, None]
    return full_state.astype(jnp.bfloat16)


def on_device(frames, w_in, w_out, skip, rates, steps_dt):
    feat_part = w_out.shape[3]
    state_part = w_in.shape[3]
    batch_n, frame_n, height, width = frames.shape[:4]
    own_chan = lax.axis_index("chan")
    out_shape = frames.shape[:4] + (feat_part,)
    rate_part = lax.dynamic_slice_in_dim(rates, own_chan * state_part, state_part, 0)
    flat_states = block_states(frames, w_in, rate_part, steps_dt)
    block_width = width * state_part
    piece = lax.all_gather(flat_states, "chan", axis=3, tiled=True)
    partitions = piece.shape[3] // block_width
    grid = piece.reshape(batch_n, frame_n, height, partitions, width, state_part)
    grid = jnp.moveaxis(grid, 3, 4).reshape(
        batch_n, frame_n, height, width, partitions * state_part
    )
    outcome = displaced_filter(pad_grid(grid), w_out, jnp.zeros(out_shape, jnp.float32))
    own_feats = lax.dynamic_slice_in_dim(frames, own_chan * feat_part, feat_part, 4)
    mixed = outcome + skip * own_feats.astype(jnp.float32)
    return mixed.astype(jnp.bfloat16)


def solution(mesh):
    return jax.shard_map(
        on_device,
        mesh=mesh,
        in_specs=(
            P(("groups", "dp"), "tm", None, None, None),
            P(None, None, None, "chan"),
            P(None, None, None, "chan"),
            P("chan"),
            P(),
            P(("groups", "dp"), "tm"),
        ),
        out_specs=P(("groups", "dp"), "tm", None, None, "chan"),
        check_vma=False,
    )
```

profile of v0, /device:TPU:0, one launch (start us, length us, event | category | flops | bytes accessed | tf_op | source)
XLA Modules:
  0.0 107.3 jit_solution(5659114071608749127)
XLA Ops:
  6.5 0.0 all-gather.2.cloned.1.call-start
  6.5 0.8 dynamic_slice.6
  7.3 0.7 fusion.117
  8.1 0.0 copy-start.4
  8.1 0.0 copy-start.6
  8.3 0.6 fusion.136
  9.0 0.0 copy-done.4
  9.0 0.0 copy-done.7
  9.0 0.0 copy-start
  9.0 0.0 copy-start.3
  9.1 0.0 copy-done.6
  9.2 0.6 add_bitcast_fusion.1
  9.9 2.4 %fusion.1 = f32[8,16,16,128]{3,2,1,0:T(8,128)S(1)} fusion(bf16[1,8,16,16,512]{4,3,2,1,0:T(8,128)(2,1)} %param.8, bf16[3,3,512,128]{3,2,1,0:T(8,128)(2,1)} %param.9), kind=kOutput, calls=%fused_computation.18 | convolution fusion | flops 268435456 | bytes 3276800 | tf_op jit(solution)/shard_map/dot_general | solution.py:26
  12.3 0.0 copy-done
  12.3 0.0 copy-done.3
  12.3 0.7 fusion.48
  13.0 0.7 fusion.45
  13.8 0.7 fusion.42
  14.5 0.7 fusion.27
  15.2 0.7 fusion.39
  15.9 0.7 fusion.36
  16.7 0.7 fusion.33
  17.4 1.6 %fusion.30 = f32[8,16,16,128]{3,2,1,0:T(8,128)S(1)} fusion(f32[8,16,16,128]{3,2,1,0:T(8,128)S(1)} %fusion.33, bf16[1,8,16,16,512]{4,3,2,1,0:T(8,128)(2,1)S(1)} %copy-done, bf16[3,3,512,128]{3,2,1,0:T(8,128)(2,1)} %param.9), kind=kOutput, calls=%fused_computation.38 | convolution fusion | flops 268697600 | bytes 4325376 | tf_op jit(solution)/shard_map/dot_general | solution.py:26
  19.0 0.0 copy-start.5
  19.0 1.1 %reshape.254 = f32[1,8,16,2048]{3,2,1,0:T(8,128)} reshape(f32[8,16,16,128]{3,2,1,0:T(8,128)S(1)} %fusion.30) | data formatting | bytes 2097152 | tf_op jit(solution)/shard_map/reshape | solution.py:40
  20.2 1.3 %broadcast_multiply_fusion = f32[1,8,16,2048]{3,2,1,0:T(8,128)S(1)} fusion(f32[1,8,16,2048]{3,2,1,0:T(8,128)} %reshape.254, f32[8,2048]{1,0:T(8,128)S(1)} %broadcast_bitcast_fusion.1), kind=kLoop, calls=%fused_computation.64 | loop fusion | flops 262144 | bytes 2162688 | tf_op jit(solution)/shard_map/mul | solution.py:47
  21.5 0.0 copy-done.5
  21.5 0.1 slice_add_fusion
  21.6 0.0 copy-done.8
  21.8 0.7 pad_maximum_fusion.1
  22.5 2.6 %pad.49 = f32[1,4,16,2048]{3,2,1,0:T(8,128)} pad(f32[1,2,16,2048]{3,2,1,0:T(8,128)} %pad_maximum_fusion.1, f32[]{:T(128)} %constant.19.clone.1), padding=0_0_0x0_1_1x0_0_0x0_0_0 | pad | bytes 786436 | tf_op jit(solution)/shard_map/pad | solution.py:46
  25.1 1.5 %pad.50 = f32[1,4,16,2048]{3,2,1,0:T(8,128)} pad(f32[1,2,16,2048]{3,2,1,0:T(8,128)S(1)} %pad_add_fusion, f32[]{:T(128)} %constant.19.clone.1), padding=0_0_0x1_0_1x0_0_0x0_0_0 | pad | bytes 786436 | tf_op jit(solution)/shard_map/pad | solution.py:46
  26.6 2.0 %add.159 = f32[1,4,16,2048]{3,2,1,0:T(8,128)} add(f32[1,4,16,2048]{3,2,1,0:T(8,128)} %pad.49, f32[1,4,16,2048]{3,2,1,0:T(8,128)} %pad.50) | non-fusion elementwise | flops 131072 | bytes 1572864 | tf_op jit(solution)/shard_map/add | solution.py:46
  28.6 1.2 %fusion.74 = f32[1,3,16,2048]{3,2,1,0:T(8,128)S(1)} fusion(f32[1,4,16,2048]{3,2,1,0:T(8,128)} %pad.50, f32[1,4,16,2048]{3,2,1,0:T(8,128)} %pad.49, f32[1,8,16,2048]{3,2,1,0:T(8,128)S(1)} %broadcast_multiply_fusion, f32[3,2048]{1,0:T(4,128)} %bitcast.235), kind=kLoop, calls=%fused_computation.66 | loop fusion | flops 294912 | bytes 1597440 | tf_op jit(solution)/shard_map/add | solution.py:32
  29.8 0.8 pad_maximum_fusion
  30.7 2.0 %pad.51 = f32[1,8,16,2048]{3,2,1,0:T(8,128)S(1)} pad(f32[1,4,16,2048]{3,2,1,0:T(8,128)} %pad_maximum_fusion, f32[]{:T(128)} %constant.19.clone.1), padding=0_0_0x0_1_1x0_0_0x0_0_0 | pad | bytes 1572868 | tf_op jit(solution)/shard_map/pad | solution.py:46
  32.6 4.1 %pad.52 = f32[1,8,16,2048]{3,2,1,0:T(8,128)} pad(f32[1,4,16,2048]{3,2,1,0:T(8,128)} %add.159, f32[]{:T(128)} %constant.19.clone.1), padding=0_0_0x1_0_1x0_0_0x0_0_0 | pad | bytes 1572868 | tf_op jit(solution)/shard_map/pad | solution.py:46
  36.7 0.9 add_bitcast_fusion
  37.7 21.5 %while.10 = (s32[]{:T(128)}, f32[1,16,2048]{2,1,0:T(8,128)S(1)}, f32[1,1,2048]{2,1,0:T(1,128)S(1)}, f32[1,16,2048]{2,1,0:T(8,128)S(1)}, s32[]{:T(128)}) while((s32[]{:T(128)}, f32[1,16,2048]{2,1,0:T(8,128)S(1)}, f32[1,1,2048]{2,1,0:T(1,128)S(1)}, f32[1,16,2048]{2,1,0:T(8,128)S(1)}, s32[]{:T(128)}) %tuple.25), condition=%wide.region_1.2_spmd, body=%wide.region_0.1_spmd.sunk | while | flops 65538 | bytes 925797 | solution.py:55
  37.7 4.9 %collective-permute-start = (f32[1,16,2048]{2,1,0:T(8,128)S(1)}, f32[1,16,2048]{2,1,0:T(8,128)S(1)}, u32[]{:S(2)}, u32[]{:S(2)}) collective-permute-start(f32[1,16,2048]{2,1,0:T(8,128)S(1)} %multiply_add_fusion.2), channel_id=1, source_target_pairs={{0,4},{4,8},{8,12},{1,5},{5,9},{9,13},{2,6},{6,10},{10,14},{3,7},{... | collective-permute-start | bytes 393224 | tf_op jit(solution)/shard_map/while/body/eval_jaxpr/ppermute | solution.py:10
  42.7 2.7 %collective-permute-done = f32[1,16,2048]{2,1,0:T(8,128)S(1)} collective-permute-done((f32[1,16,2048]{2,1,0:T(8,128)S(1)}, f32[1,16,2048]{2,1,0:T(8,128)S(1)}, u32[]{:S(2)}, u32[]{:S(2)}) %collective-permute-start) | collective-permute-done | bytes 131104 | tf_op jit(solution)/shard_map/while/body/eval_jaxpr/ppermute | solution.py:10
  45.4 4.4 %collective-permute-start = (f32[1,16,2048]{2,1,0:T(8,128)S(1)}, f32[1,16,2048]{2,1,0:T(8,128)S(1)}, u32[]{:S(2)}, u32[]{:S(2)}) collective-permute-start(f32[1,16,2048]{2,1,0:T(8,128)S(1)} %multiply_add_fusion.2), channel_id=1, source_target_pairs={{0,4},{4,8},{8,12},{1,5},{5,9},{9,13},{2,6},{6,10},{10,14},{3,7},{... | collective-permute-start | bytes 393224 | tf_op jit(solution)/shard_map/while/body/eval_jaxpr/ppermute | solution.py:10
  49.8 2.5 %collective-permute-done = f32[1,16,2048]{2,1,0:T(8,128)S(1)} collective-permute-done((f32[1,16,2048]{2,1,0:T(8,128)S(1)}, f32[1,16,2048]{2,1,0:T(8,128)S(1)}, u32[]{:S(2)}, u32[]{:S(2)}) %collective-permute-start) | collective-permute-done | bytes 131104 | tf_op jit(solution)/shard_map/while/body/eval_jaxpr/ppermute | solution.py:10
  52.4 4.4 %collective-permute-start = (f32[1,16,2048]{2,1,0:T(8,128)S(1)}, f32[1,16,2048]{2,1,0:T(8,128)S(1)}, u32[]{:S(2)}, u32[]{:S(2)}) collective-permute-start(f32[1,16,2048]{2,1,0:T(8,128)S(1)} %multiply_add_fusion.2), channel_id=1, source_target_pairs={{0,4},{4,8},{8,12},{1,5},{5,9},{9,13},{2,6},{6,10},{10,14},{3,7},{... | collective-permute-start | bytes 393224 | tf_op jit(solution)/shard_map/while/body/eval_jaxpr/ppermute | solution.py:10
  56.7 2.5 %collective-permute-done = f32[1,16,2048]{2,1,0:T(8,128)S(1)} collective-permute-done((f32[1,16,2048]{2,1,0:T(8,128)S(1)}, f32[1,16,2048]{2,1,0:T(8,128)S(1)}, u32[]{:S(2)}, u32[]{:S(2)}) %collective-permute-start) | collective-permute-done | bytes 131104 | tf_op jit(solution)/shard_map/while/body/eval_jaxpr/ppermute | solution.py:10
  59.2 2.2 %add_convert_fusion = bf16[1,8,16,2048]{3,2,1,0:T(8,128)(2,1)} fusion(f32[1,8,16,2048]{3,2,1,0:T(8,128)S(1)} %pad.51, f32[1,8,16,2048]{3,2,1,0:T(8,128)} %pad.52, f32[16,2048]{1,0:T(8,128)S(1)} %bitcast.230, f32[8,2048]{1,0:T(8,128)} %add_bitcast_fusion.1), kind=kLoop, calls=%fused_computation.61 | loop fusion | flops 1048576 | bytes 2818048 | tf_op jit(solution)/shard_map/convert_element_type | solution.py:57
  61.4 0.0 all-gather.2.cloned.1.call-update
  61.5 23.6 %all-gather.2.cloned.1.call-done = bf16[1,8,16,4096]{3,2,1,0:T(8,128)(2,1)} async-done(((bf16[1,8,16,2048]{3,2,1,0:T(8,128)(2,1)}), bf16[1,8,16,4096]{3,2,1,0:T(8,128)(2,1)}) %all-gather.2.cloned.1.call-update) | async-done | bytes 1048592 | tf_op jit(solution)/shard_map/all_gather | solution.py:69
  85.0 1.5 %copy.26 = bf16[16,8,32,128]{3,2,1,0:T(8,128)(2,1)S(1)} copy(bf16[16,8,32,128]{3,1,2,0:T(8,128)(2,1)} %bitcast.232) | data formatting | bytes 2097152
  86.5 1.9 %copy.28 = bf16[1,8,16,2,16,128]{5,3,4,2,1,0:T(2,128)(2,1)} copy(bf16[1,8,16,2,16,128]{5,4,3,2,1,0:T(8,128)(2,1)S(1)} %bitcast.231) | data formatting | bytes 2097152 | tf_op jit(solution)/shard_map/reshape | solution.py:71
  88.4 1.7 %reshape.256 = bf16[1,8,16,16,256]{4,3,2,1,0:T(8,128)(2,1)S(1)} reshape(bf16[1,8,16,16,2,128]{5,4,3,2,1,0:T(2,128)(2,1)} %bitcast.228) | data formatting | bytes 2097152 | tf_op jit(solution)/shard_map/reshape | solution.py:72
  90.1 2.5 %dot_general.116 = bf16[8,16,16,256]{3,2,1,0:T(8,128)(2,1)} reshape(bf16[1,8,16,16,2,128]{5,4,3,2,1,0:T(2,128)(2,1)} %bitcast.229) | data formatting | bytes 2097152 | tf_op jit(solution)/shard_map/dot_general | solution.py:26
  92.7 1.4 %fusion.55 = f32[8,16,16,256]{3,2,1,0:T(8,128)S(1)} fusion(bf16[1,8,16,16,256]{4,3,2,1,0:T(8,128)(2,1)S(1)} %reshape.256, bf16[3,3,256,256]{3,2,1,0:T(8,128)(2,1)} %param.10), kind=kOutput, calls=%fused_computation.48 | convolution fusion | flops 268435456 | bytes 3276800 | tf_op jit(solution)/shard_map/dot_general | solution.py:26
  94.1 0.5 fusion.58
  94.5 0.5 fusion.61
  95.0 0.5 fusion.64
  95.5 0.4 fusion.67
  95.9 0.4 fusion.70
  96.4 0.0 copy-start.1
  96.4 0.4 fusion.52
  96.8 0.8 copy-done.1
  97.6 0.4 fusion.82
  98.0 0.2 copy-done.10
  98.3 2.2 %fusion.24 = bf16[1,8,16,16,256]{4,3,2,1,0:T(8,128)(2,1)} fusion(f32[8,16,16,256]{3,2,1,0:T(8,128)S(1)} %fusion.70, f32[8,16,16,256]{3,2,1,0:T(8,128)S(1)} %fusion.67, f32[8,16,16,256]{3,2,1,0:T(8,128)S(1)} %fusion.64, f32[8,16,16,256]{3,2,1,0:T(8,128)S(1)} %fusion.82, f32[8,16,16,256]{3,2,1,0:T(8,128)S(1)} %fusion.61, f32[8,16,16,256]{3,2,1,0:T(8,128)S(1)} %fusion.58, ...), kind=kOutput, calls=%fused_computation.34 | convolution fusion | flops 274726912 | bytes 20055044 | tf_op jit(solution)/shard_map/dot_general | solution.py:26
  (37 shorter events, 0.6 us)
Async XLA Ops:
  6.5 78.5 %all-gather.2.cloned.1.call-start = ((), (), s32[]{:S(2)}) async-start(), calls=%async_computation | async-start | bytes 1572864 | tf_op jit(solution)/shard_map/all_gather | solution.py:69
  8.1 0.9 copy-start.4
  8.1 1.0 copy-start.6
  8.2 0.8 copy-start.7
  9.0 3.3 %copy-start = (bf16[1,8,16,16,512]{4,3,2,1,0:T(8,128)(2,1)S(1)}, bf16[1,8,16,16,512]{4,3,2,1,0:T(8,128)(2,1)}, u32[]{:S(2)}) copy-start(bf16[1,8,16,16,512]{4,3,2,1,0:T(8,128)(2,1)} %param.8) | copy-start | bytes 6291460
  9.0 3.3 %copy-start.3 = (bf16[3,3,512,128]{3,2,1,0:T(8,128)(2,1)S(1)}, bf16[3,3,512,128]{3,2,1,0:T(8,128)(2,1)}, u32[]{:S(2)}) copy-start(bf16[3,3,512,128]{3,2,1,0:T(8,128)(2,1)} %param.9) | copy-start | bytes 3538948
  19.0 2.5 %copy-start.5 = (f32[1,4,1,2048]{3,1,2,0:T(4,128)S(1)}, f32[1,4,1,2048]{3,1,2,0:T(4,128)}, u32[]{:S(2)}) copy-start(f32[1,4,1,2048]{3,1,2,0:T(4,128)} %copy-done.4) | copy-start | bytes 98308
  20.2 1.4 %copy-start.8 = (f32[1,2,1,2048]{3,1,2,0:T(2,128)S(1)}, f32[1,2,1,2048]{3,1,2,0:T(2,128)}, u32[]{:S(2)}) copy-start(f32[1,2,1,2048]{3,1,2,0:T(2,128)} %copy-done.7) | copy-start | bytes 49156
  20.2 1.5 %copy-start.9 = (f32[1,1,1,2048]{3,1,2,0:T(1,128)S(1)}, f32[1,1,1,2048]{3,1,2,0:T(1,128)}, u32[]{:S(2)}) copy-start(f32[1,1,1,2048]{3,1,2,0:T(1,128)} %get-tuple-element.45) | copy-start | bytes 24580
  37.7 7.7 %collective-permute-start = (f32[1,16,2048]{2,1,0:T(8,128)S(1)}, f32[1,16,2048]{2,1,0:T(8,128)S(1)}, u32[]{:S(2)}, u32[]{:S(2)}) collective-permute-start(f32[1,16,2048]{2,1,0:T(8,128)S(1)} %multiply_add_fusion.2), channel_id=1, source_target_pairs={{0,4},{4,8},{8,12},{1,5},{5,9},{9,13},{2,6},{6,10},{10,14},{3,7},{... | collective-permute-start | bytes 393224 | tf_op jit(solution)/shard_map/while/body/eval_jaxpr/ppermute | solution.py:10
  45.4 6.9 %collective-permute-start = (f32[1,16,2048]{2,1,0:T(8,128)S(1)}, f32[1,16,2048]{2,1,0:T(8,128)S(1)}, u32[]{:S(2)}, u32[]{:S(2)}) collective-permute-start(f32[1,16,2048]{2,1,0:T(8,128)S(1)} %multiply_add_fusion.2), channel_id=1, source_target_pairs={{0,4},{4,8},{8,12},{1,5},{5,9},{9,13},{2,6},{6,10},{10,14},{3,7},{... | collective-permute-start | bytes 393224 | tf_op jit(solution)/shard_map/while/body/eval_jaxpr/ppermute | solution.py:10
  52.4 6.9 %collective-permute-start = (f32[1,16,2048]{2,1,0:T(8,128)S(1)}, f32[1,16,2048]{2,1,0:T(8,128)S(1)}, u32[]{:S(2)}, u32[]{:S(2)}) collective-permute-start(f32[1,16,2048]{2,1,0:T(8,128)S(1)} %multiply_add_fusion.2), channel_id=1, source_target_pairs={{0,4},{4,8},{8,12},{1,5},{5,9},{9,13},{2,6},{6,10},{10,14},{3,7},{... | collective-permute-start | bytes 393224 | tf_op jit(solution)/shard_map/while/body/eval_jaxpr/ppermute | solution.py:10
  92.7 1.4 %copy-start.2 = (bf16[3,3,256,256]{3,2,1,0:T(8,128)(2,1)S(1)}, bf16[3,3,256,256]{3,2,1,0:T(8,128)(2,1)}, u32[]{:S(2)}) copy-start(bf16[3,3,256,256]{3,2,1,0:T(8,128)(2,1)} %param.10) | copy-start | bytes 3538948
  96.4 1.2 %copy-start.1 = (bf16[8,16,16,256]{3,2,1,0:T(8,128)(2,1)S(1)}, bf16[8,16,16,256]{3,2,1,0:T(8,128)(2,1)}, u32[]{:S(2)}) copy-start(bf16[8,16,16,256]{3,2,1,0:T(8,128)(2,1)} %dot_general.116) | copy-start | bytes 3145732
  97.6 0.7 copy-start.10
Sparse Core Ops, SparseCore 0:
  61.6 23.3 all-gather.1
where the time goes:
time: 108 us; the launch traced here: 107 us
  waiting for transfers between devices  31.3 us (29%)
  local copies, waits for them, and re-layouts  21 us (19%)
  matrix products  15.8 us (15%)
  between operations  13.8 us (13%)
  starting transfers between devices  13.7 us (13%)
  other arithmetic  11.6 us (11%)
    all_gather x1, waiting for transfers between devices, on_device(): piece = lax.all_gather(flat_states, 'chan', axis=3, tiled=True)  23.6 us
    dot_general x18, matrix products, displaced_filter(): jnp.dot(window, weight[row_off, col_off], preferred_element_type=jnp.floa...  15.8 us
    ppermute x3, starting transfers between devices, from_behind(): return lax.ppermute(block, axis, route)  13.7 us
    pad x8, local copies, waits for them, and re-layouts, block_states(): lax.associative_scan(combine_operator, (decay_flat, gain_flat * flat_driv...  10.3 us
    ppermute x3, waiting for transfers between devices, from_behind(): return lax.ppermute(block, axis, route)  7.73 us
    dot_general x1, local copies, waits for them, and re-layouts, displaced_filter(): jnp.dot(window, weight[row_off, col_off], preferred_element_type=jnp.floa...  2.52 us
    unnamed x23, local copies, waits for them, and re-layouts  2.51 us
    convert_element_type x1, other arithmetic, block_states(): return full_state.astype(jnp.bfloat16)  2.21 us
  transfers between devices with their start and end apart: 4, of which 4 were waited for; matrix products, arithmetic and copies ran while one was open for 0% of the time, Pallas kernels for 0%

commit v1 on v0

--- a/solution.py
+++ b/solution.py
@@ -1,6 +1,10 @@
+import functools
+
 import jax
 import jax.numpy as jnp
 from jax import lax
+from jax.experimental import pallas as pl
+from jax.experimental.pallas import tpu as pltpu
 from jax.sharding import PartitionSpec as P
 
 
@@ -78,9 +82,352 @@
     return mixed.astype(jnp.bfloat16)
 
 
+LANES = 128
+MESH = pl.DeviceIdType.MESH
+
+
+def fused_kernel(
+    dims,
+    frames_hbm,
+    w_in_hbm,
+    w_out_hbm,
+    skip_ref,
+    rates_ref,
+    steps_ref,
+    out_hbm,
+    frames_buf,
+    w_in_buf,
+    w_out_buf,
+    out_buf,
+    states,
+    running,
+    ends,
+    block_decay,
+    carry,
+    taps,
+    frame_sem,
+    w_in_sem,
+    w_out_sem,
+    out_sem,
+    state_send,
+    state_recv,
+    end_send,
+    end_recv,
+    decay_send,
+    decay_recv,
+    carry_send,
+    carry_recv,
+):
+    blocks, count, height, width, group = dims
+    cells = height * width
+    rows = group * cells
+    groups_n = count // group
+    part = running.shape[1]
+    feats = out_buf.shape[1]
+    chans = 2 * part
+    me = lax.axis_index("chan")
+    other = 1 - me
+    z = lax.axis_index("tm")
+
+    def frame_copy(g):
+        span = pl.ds(pl.multiple_of(g * rows, rows), rows)
+        return pltpu.make_async_copy(
+            frames_hbm.at[span], frames_buf.at[span], frame_sem.at[g]
+        )
+
+    def w_in_copy(tap):
+        row_off, col_off = tap // 3, tap % 3
+        place = (col_off * 3 + row_off) * part
+        return pltpu.make_async_copy(
+            w_in_hbm.at[tap], w_in_buf.at[:, place : place + part], w_in_sem.at[tap]
+        )
+
+    def out_copy(g):
+        span = pl.ds(pl.multiple_of(g * rows, rows), rows)
+        return pltpu.make_async_copy(out_buf.at[span], out_hbm.at[span], out_sem.at[g])
+
+    w_out_copy = pltpu.make_async_copy(w_out_hbm, w_out_buf, w_out_sem)
+    for tap in range(9):
+        w_in_copy(tap).start()
+    for g in range(groups_n):
+        frame_copy(g).start()
+    w_out_copy.start()
+
+    barrier = pltpu.get_barrier_semaphore()
+    pl.semaphore_signal(barrier, inc=1, device_id={"chan": other}, device_id_type=MESH)
+    for k in range(blocks):
+
+        @pl.when(k != z)
+        def _():
+            pl.semaphore_signal(barrier, inc=1, device_id={"tm": k}, device_id_type=MESH)
+
+    rates_all = rates_ref[...]
+    rates_own = rates_ref[:, pl.ds(pl.multiple_of(me * part, part), part)]
+    total = steps_ref[0, 0]
+    for t in range(1, count):
+        total = total + steps_ref[0, t]
+    block_decay[z] = jnp.broadcast_to(jnp.exp(-rates_own * total), (8, part))
+    running[...] = jnp.zeros_like(running)
+    taps[...] = jnp.zeros_like(taps)
+    pl.semaphore_wait(barrier, blocks)
+
+    def decay_send_to(k):
+        return pltpu.make_async_remote_copy(
+            src_ref=block_decay.at[z],
+            dst_ref=block_decay.at[z],
+            send_sem=decay_send.at[k],
+            recv_sem=decay_recv.at[z],
+            device_id={"tm": k},
+            device_id_type=MESH,
+        )
+
+    def decay_from(k):
+        return pltpu.make_async_remote_copy(
+            src_ref=block_decay.at[k],
+            dst_ref=block_decay.at[k],
+            send_sem=decay_send.at[k],
+            recv_sem=decay_recv.at[k],
+            device_id={"tm": k},
+            device_id_type=MESH,
+        )
+
+    def end_send_to(k):
+        return pltpu.make_async_remote_copy(
+            src_ref=states.at[me, count - 1],
+            dst_ref=ends.at[z],
+            send_sem=end_send.at[k],
+            recv_sem=end_recv.at[z],
+            device_id={"tm": k},
+            device_id_type=MESH,
+        )
+
+    def end_from(k):
+        return pltpu.make_async_remote_copy(
+            src_ref=states.at[me, count - 1],
+            dst_ref=ends.at[k],
+            send_sem=end_send.at[k],
+            recv_sem=end_recv.at[k],
+            device_id={"tm": k},
+            device_id_type=MESH,
+        )
+
+    def state_copy(side, t):
+        return pltpu.make_async_remote_copy(
+            src_ref=states.at[side, t],
+            dst_ref=states.at[side, t],
+            send_sem=state_send.at[t],
+            recv_sem=state_recv.at[t],
+            device_id={"chan": other},
+            device_id_type=MESH,
+        )
+
+    def carry_copy(side):
+        return pltpu.make_async_remote_copy(
+            src_ref=carry.at[side],
+            dst_ref=carry.at[side],
+            send_sem=carry_send,
+            recv_sem=carry_recv,
+            device_id={"chan": other},
+            device_id_type=MESH,
+        )
+
+    for k in range(1, blocks):
+
+        @pl.when(z < k)
+        def _():
+            decay_send_to(k).start()
+
+    for tap in range(9):
+        w_in_copy(tap).wait()
+
+    column = lax.broadcasted_iota(jnp.int32, (cells, 1), 0) % width
+    first_col = column == 0
+    last_col = column == width - 1
+
+    def drive_step(g, unused):
+        frame_copy(g).wait()
+        span = pl.ds(pl.multiple_of(g * rows, rows), rows)
+        product = jnp.dot(
+            frames_buf[span, :], w_in_buf[...], preferred_element_type=jnp.float32
+        )
+        for f in range(group):
+            t = g * group + f
+            mine = product[f * cells : (f + 1) * cells]
+            sums = []
+            for col_off in range(3):
+                base = col_off * 3 * part
+                above = mine[:, base : base + part]
+                level = mine[:, base + part : base + 2 * part]
+                below = mine[:, base + 2 * part : base + 3 * part]
+                zero = jnp.zeros((width, part), jnp.float32)
+                sums.append(
+                    level
+                    + jnp.concatenate([zero, above[: cells - width]], axis=0)
+                    + jnp.concatenate([below[width:], zero], axis=0)
+                )
+            drive = (
+                sums[1]
+                + jnp.where(first_col, 0.0, pltpu.roll(sums[0], 1, 0))
+                + jnp.where(last_col, 0.0, pltpu.roll(sums[2], cells - 1, 0))
+            )
+            scaled = rates_own * steps_ref[0, t]
+            decay = jnp.exp(-scaled)
+            gain_in = (1.0 - decay) / rates_own
+            state = decay * running[...] + gain_in * drive
+            running[...] = state
+            states[me, t] = state.astype(jnp.bfloat16)
+            state_copy(me, t).start()
+        return unused
+
+    lax.fori_loop(0, groups_n, drive_step, 0)
+
+    for k in reversed(range(1, blocks)):
+
+        @pl.when(z < k)
+        def _():
+            end_send_to(k).start()
+
+    running[...] = jnp.zeros_like(running)
+    for k in range(blocks - 1):
+
+        @pl.when(k < z)
+        def _():
+            decay_from(k).wait_recv()
+            end_from(k).wait_recv()
+            running[...] = block_decay[k][:1] * running[...] + ends[k].astype(jnp.float32)
+
+    carry[me] = running[...].astype(jnp.bfloat16)
+    carry_copy(me).start()
+    w_out_copy.wait()
+    carry_copy(other).wait_recv()
+
+    own_feats = pl.ds(pl.multiple_of(me * feats, feats), feats)
+
+    def mix_step(g, elapsed):
+        span = pl.ds(pl.multiple_of(g * rows, rows), rows)
+        for f in range(group):
+            t = g * group + f
+            state_copy(other, t).wait_recv()
+            elapsed = elapsed + steps_ref[0, t]
+            product = jnp.exp(-rates_all * elapsed)
+            for side in range(2):
+                lanes = slice(side * part, (side + 1) * part)
+                state = states[side, t].astype(jnp.float32) + product[:, lanes] * carry[
+                    side
+                ].astype(jnp.float32)
+                state = state.astype(jnp.bfloat16).astype(jnp.float32)
+                held = (
+                    jnp.where(first_col, 0.0, pltpu.roll(state, 1, 0)),
+                    state,
+                    jnp.where(last_col, 0.0, pltpu.roll(state, cells - 1, 0)),
+                )
+                for col_off in range(3):
+                    at = col_off * chans + side * part
+                    taps[f, width : width + cells, at : at + part] = held[col_off].astype(
+                        jnp.bfloat16
+                    )
+        result = None
+        for row_off in range(3):
+            window = taps[:, row_off * width : row_off * width + cells, :].reshape(rows, 3 * chans)
+            term = jnp.dot(
+                window,
+                w_out_buf[row_off * 3 * chans : (row_off + 1) * 3 * chans, :],
+                preferred_element_type=jnp.float32,
+            )
+            result = term if result is None else result + term
+        result = result + skip_ref[...] * frames_buf[span, own_feats].astype(jnp.float32)
+        out_buf[span, :] = result.astype(jnp.bfloat16)
+        out_copy(g).start()
+        return elapsed
+
+    lax.fori_loop(0, groups_n, mix_step, jnp.float32(0.0))
+
+    for g in range(groups_n):
+        out_copy(g).wait()
+    for t in range(count):
+        state_copy(me, t).wait_send()
+    carry_copy(me).wait_send()
+    for k in range(1, blocks):
+
+        @pl.when(z < k)
+        def _():
+            decay_send_to(k).wait_send()
+            end_send_to(k).wait_send()
+
+
+def on_device_fused(frames, w_in, w_out, skip, rates, steps_dt):
+    _, count, height, width, feats_in = frames.shape
+    part, feats = w_in.shape[3], w_out.shape[3]
+    chans = w_out.shape[2]
+    blocks = lax.axis_size("tm")
+    cells = height * width
+    group = 2
+    groups_n = count // group
+    dims = (blocks, count, height, width, group)
+    hbm = pl.BlockSpec(memory_space=pltpu.HBM)
+    vmem = pl.BlockSpec(memory_space=pltpu.VMEM)
+    smem = pl.BlockSpec(memory_space=pltpu.SMEM)
+    dma = pltpu.SemaphoreType.DMA
+    out = pl.pallas_call(
+        functools.partial(fused_kernel, dims),
+        out_shape=jax.ShapeDtypeStruct((count * cells, feats), jnp.bfloat16),
+        in_specs=[hbm, hbm, hbm, vmem, vmem, smem],
+        out_specs=pl.BlockSpec(memory_space=pl.ANY),
+        scratch_shapes=[
+            pltpu.VMEM((count * cells, feats_in), jnp.bfloat16),
+            pltpu.VMEM((feats_in, 9 * part), jnp.bfloat16),
+            pltpu.VMEM((9 * chans, feats), jnp.bfloat16),
+            pltpu.VMEM((count * cells, feats), jnp.bfloat16),
+            pltpu.VMEM((2, count, cells, part), jnp.bfloat16),
+            pltpu.VMEM((cells, part), jnp.float32),
+            pltpu.VMEM((blocks, cells, part), jnp.bfloat16),
+            pltpu.VMEM((blocks, 8, part), jnp.float32),
+            pltpu.VMEM((2, cells, part), jnp.bfloat16),
+            pltpu.VMEM((group, cells + 2 * width, 3 * chans), jnp.bfloat16),
+            dma((groups_n,)),
+            dma((9,)),
+            dma,
+            dma((groups_n,)),
+            dma((count,)),
+            dma((count,)),
+            dma((blocks,)),
+            dma((blocks,)),
+            dma((blocks,)),
+            dma((blocks,)),
+            dma,
+            dma,
+        ],
+        compiler_params=pltpu.CompilerParams(
+            collective_id=0, has_side_effects=True, vmem_limit_bytes=48 << 20
+        ),
+    )(
+        frames.reshape(count * cells, feats_in),
+        w_in.reshape(9, feats_in, part),
+        w_out.reshape(9 * chans, feats),
+        skip.reshape(1, feats),
+        rates.reshape(1, chans),
+        steps_dt,
+    )
+    return out.reshape(1, count, height, width, feats)
+
+
+def pick(mesh, frames, w_in, w_out, skip, rates, steps_dt):
+    clips, count, height, width = frames.shape[:4]
+    fused = (
+        mesh.shape["chan"] == 2
+        and clips == 1
+        and count % 2 == 0
+        and width == 16
+        and w_in.shape[3] == LANES
+        and w_out.shape[3] % LANES == 0
+    )
+    body = on_device_fused if fused else on_device
+    return body(frames, w_in, w_out, skip, rates, steps_dt)
+
+
 def solution(mesh):
     return jax.shard_map(
-        on_device,
+        functools.partial(pick, mesh),
         mesh=mesh,
         in_specs=(
             P(("groups", "dp"), "tm", None, None, None),

time: 108 us -> 33.1 us (0.31)
  waiting for transfers between devices: 31.3 us -> 0 us
  Pallas kernels: 0 us -> 25.8 us
  matrix products: 15.8 us -> 0 us
  local copies, waits for them, and re-layouts: 21 us -> 7.11 us
  between operations: 13.8 us -> 0.02 us
  starting transfers between devices: 13.7 us -> 0 us
  other arithmetic: 11.6 us -> 0 us
    pallas_call x0 -> x1, Pallas kernels: none -> 25.8 us  [on_device_fused(): pl.pallas_call(functools.partial(fused_kernel, dims), out_shape=jax.Shape...]
    all_gather x1 -> x0, waiting for transfers between devices: 23.6 us -> none  [on_device(): piece = lax.all_gather(flat_states, 'chan', axis=3, tiled=True)]
    dot_general x18 -> x0, matrix products: 15.8 us -> none  [displaced_filter(): jnp.dot(window, weight[row_off, col_off], preferred_element_type=jnp.floa...]
    ppermute x3 -> x0, starting transfers between devices: 13.7 us -> none  [from_behind(): return lax.ppermute(block, axis, route)]
    pad x8 -> x0, local copies, waits for them, and re-layouts: 10.3 us -> none  [block_states(): lax.associative_scan(combine_operator, (decay_flat, gain_flat * flat_driv...]
    ppermute x3 -> x0, waiting for transfers between devices: 7.73 us -> none  [from_behind(): return lax.ppermute(block, axis, route)]
    reshape x3 -> x0, local copies, waits for them, and re-layouts: 4.78 us -> none  [the longest x1 1.91 us: on_device(): piece.reshape(batch_n, frame_n, height, partitions, width, state_part)]
    unnamed x23 -> x13, local copies, waits for them, and re-layouts: 2.51 us -> 7.11 us
  transfers between devices with their start and end apart: 4 -> 0, of which waited for: 4 -> 0; matrix products, arithmetic and copies ran while one was open for 0% -> 0% of each run, Pallas kernels for 0% -> 0%
where the time goes in v1:
time: 33.1 us; the launch traced here: 32.9 us
  Pallas kernels  25.8 us (78%)
  local copies, waits for them, and re-layouts  7.11 us (21%)
    pallas_call x1, Pallas kernels, on_device_fused(): pl.pallas_call(functools.partial(fused_kernel, dims), out_shape=jax.Shape...  25.8 us
    unnamed x13, local copies, waits for them, and re-layouts  7.11 us

profile of v1, /device:TPU:0, one launch (start us, length us, event | category | flops | bytes accessed | tf_op | source)
XLA Modules:
  0.0 32.9 jit_solution(10781086751355535148)
XLA Ops:
  0.0 0.0 copy-start
  0.0 1.6 %copy-done = bf16[1,8,16,16,512]{4,3,2,1,0:T(8,128)(2,1)S(1)} copy-done((bf16[1,8,16,16,512]{4,3,2,1,0:T(8,128)(2,1)S(1)}, bf16[1,8,16,16,512]{4,3,2,1,0:T(8,128)(2,1)}, u32[]{:S(2)}) %copy-start) | copy-done | bytes 2097176
  1.6 0.0 copy-start.1
  1.6 1.3 %copy-done.1 = bf16[3,3,512,128]{3,2,1,0:T(8,128)(2,1)S(1)} copy-done((bf16[3,3,512,128]{3,2,1,0:T(8,128)(2,1)S(1)}, bf16[3,3,512,128]{3,2,1,0:T(8,128)(2,1)}, u32[]{:S(2)}) %copy-start.1) | copy-done | bytes 1179672
  2.9 0.0 copy-start.2
  2.9 1.3 %copy-done.2 = bf16[3,3,256,256]{3,2,1,0:T(8,128)(2,1)S(1)} copy-done((bf16[3,3,256,256]{3,2,1,0:T(8,128)(2,1)S(1)}, bf16[3,3,256,256]{3,2,1,0:T(8,128)(2,1)}, u32[]{:S(2)}) %copy-start.2) | copy-done | bytes 1179672
  4.1 0.0 copy-start.3
  4.1 0.7 %copy-done.3 = f32[256]{0:T(256)S(1)} copy-done((f32[256]{0:T(256)S(1)}, f32[256]{0:T(256)}, u32[]{:S(2)}) %copy-start.3) | copy-done | bytes 1048
  4.8 0.0 copy-start.4
  4.8 0.7 %copy-done.4 = f32[256]{0:T(256)S(1)} copy-done((f32[256]{0:T(256)S(1)}, f32[256]{0:T(256)}, u32[]{:S(2)}) %copy-start.4) | copy-done | bytes 1048
  5.5 0.0 copy-start.5
  5.5 0.7 %copy-done.5 = f32[1,8]{1,0:T(1,128)S(1)} copy-done((f32[1,8]{1,0:T(1,128)S(1)}, f32[1,8]{1,0:T(1,128)}, u32[]{:S(2)}) %copy-start.5) | copy-done | bytes 56
  6.1 25.8 %shard_map.64 = bf16[2048,256]{1,0:T(8,128)(2,1)S(1)} custom-call(bf16[2048,512]{1,0:T(8,128)(2,1)S(1)} %bitcast.7, bf16[9,512,128]{2,1,0:T(8,128)(2,1)S(1)} %bitcast.8, bf16[2304,256]{1,0:T(8,128)(2,1)S(1)} %bitcast.9, f32[1,256]{1,0:T(1,128)S(1)} %bitcast.10, f32[1,256]{1,0:T(1,128)S(1)} %bitcast.11, f32[1,8]{1,0:T(1,128)S(1)} %copy-done.5), custom_call_target="tpu_custom_call" | custom-call | tf_op jit(solution)/shard_map/pallas_call | solution.py:371
  31.9 1.0 %copy.8 = bf16[1,8,16,16,256]{4,3,2,1,0:T(8,128)(2,1)} copy(bf16[1,8,16,16,256]{4,3,2,1,0:T(8,128)(2,1)S(1)} %bitcast.6) | data formatting | bytes 2097152
Async XLA Ops:
  0.0 1.6 %copy-start = (bf16[1,8,16,16,512]{4,3,2,1,0:T(8,128)(2,1)S(1)}, bf16[1,8,16,16,512]{4,3,2,1,0:T(8,128)(2,1)}, u32[]{:S(2)}) copy-start(bf16[1,8,16,16,512]{4,3,2,1,0:T(8,128)(2,1)} %param.6) | copy-start | bytes 6291460
  1.6 1.3 %copy-start.1 = (bf16[3,3,512,128]{3,2,1,0:T(8,128)(2,1)S(1)}, bf16[3,3,512,128]{3,2,1,0:T(8,128)(2,1)}, u32[]{:S(2)}) copy-start(bf16[3,3,512,128]{3,2,1,0:T(8,128)(2,1)} %param.7) | copy-start | bytes 3538948
  2.9 1.3 %copy-start.2 = (bf16[3,3,256,256]{3,2,1,0:T(8,128)(2,1)S(1)}, bf16[3,3,256,256]{3,2,1,0:T(8,128)(2,1)}, u32[]{:S(2)}) copy-start(bf16[3,3,256,256]{3,2,1,0:T(8,128)(2,1)} %param.8) | copy-start | bytes 3538948
  4.1 0.7 %copy-start.3 = (f32[256]{0:T(256)S(1)}, f32[256]{0:T(256)}, u32[]{:S(2)}) copy-start(f32[256]{0:T(256)} %param.9) | copy-start | bytes 3076
  4.8 0.7 %copy-start.4 = (f32[256]{0:T(256)S(1)}, f32[256]{0:T(256)}, u32[]{:S(2)}) copy-start(f32[256]{0:T(256)} %param.10) | copy-start | bytes 3076
  5.5 0.7 %copy-start.5 = (f32[1,8]{1,0:T(1,128)S(1)}, f32[1,8]{1,0:T(1,128)}, u32[]{:S(2)}) copy-start(f32[1,8]{1,0:T(1,128)} %steps_ref.1) | copy-start | bytes 100

commit v2 on v1

--- a/solution.py
+++ b/solution.py
@@ -91,10 +91,13 @@
     frames_hbm,
     w_in_hbm,
     w_out_hbm,
+    skip_hbm,
+    rates_hbm,
+    steps_hbm,
+    out_hbm,
     skip_ref,
     rates_ref,
     steps_ref,
-    out_hbm,
     frames_buf,
     w_in_buf,
     w_out_buf,
@@ -117,6 +120,7 @@
     decay_recv,
     carry_send,
     carry_recv,
+    small_sem,
 ):
     blocks, count, height, width, group = dims
     cells = height * width
@@ -147,6 +151,13 @@
         return pltpu.make_async_copy(out_buf.at[span], out_hbm.at[span], out_sem.at[g])
 
     w_out_copy = pltpu.make_async_copy(w_out_hbm, w_out_buf, w_out_sem)
+    small = [
+        pltpu.make_async_copy(steps_hbm, steps_ref, small_sem.at[0]),
+        pltpu.make_async_copy(rates_hbm, rates_ref, small_sem.at[1]),
+        pltpu.make_async_copy(skip_hbm, skip_ref, small_sem.at[2]),
+    ]
+    for copy in small:
+        copy.start()
     for tap in range(9):
         w_in_copy(tap).start()
     for g in range(groups_n):
@@ -161,6 +172,8 @@
         def _():
             pl.semaphore_signal(barrier, inc=1, device_id={"tm": k}, device_id_type=MESH)
 
+    for copy in small:
+        copy.wait()
     rates_all = rates_ref[...]
     rates_own = rates_ref[:, pl.ds(pl.multiple_of(me * part, part), part)]
     total = steps_ref[0, 0]
@@ -365,15 +378,16 @@
     groups_n = count // group
     dims = (blocks, count, height, width, group)
     hbm = pl.BlockSpec(memory_space=pltpu.HBM)
-    vmem = pl.BlockSpec(memory_space=pltpu.VMEM)
-    smem = pl.BlockSpec(memory_space=pltpu.SMEM)
     dma = pltpu.SemaphoreType.DMA
     out = pl.pallas_call(
         functools.partial(fused_kernel, dims),
         out_shape=jax.ShapeDtypeStruct((count * cells, feats), jnp.bfloat16),
-        in_specs=[hbm, hbm, hbm, vmem, vmem, smem],
+        in_specs=[hbm] * 6,
         out_specs=pl.BlockSpec(memory_space=pl.ANY),
         scratch_shapes=[
+            pltpu.VMEM((1, feats), jnp.float32),
+            pltpu.VMEM((1, chans), jnp.float32),
+            pltpu.SMEM((1, count), jnp.float32),
             pltpu.VMEM((count * cells, feats_in), jnp.bfloat16),
             pltpu.VMEM((feats_in, 9 * part), jnp.bfloat16),
             pltpu.VMEM((9 * chans, feats), jnp.bfloat16),
@@ -396,9 +410,10 @@
             dma((blocks,)),
             dma,
             dma,
+            dma((3,)),
         ],
         compiler_params=pltpu.CompilerParams(
-            collective_id=0, has_side_effects=True, vmem_limit_bytes=48 << 20
+            collective_id=0, has_side_effects=True, vmem_limit_bytes=62 << 20
         ),
     )(
         frames.reshape(count * cells, feats_in),

time: 33.1 us -> 27.7 us (0.84)
  local copies, waits for them, and re-layouts: 7.11 us -> 2.26 us
  Pallas kernels: 25.8 us -> 25.3 us
    unnamed x13 -> x1, local copies, waits for them, and re-layouts: 7.11 us -> 2.26 us
    pallas_call x1, Pallas kernels: 25.8 us -> 25.3 us  [on_device_fused(): pl.pallas_call(functools.partial(fused_kernel, dims), out_shape=jax.Shape...]
where the time goes in v2:
time: 27.7 us; the launch traced here: 27.5 us
  Pallas kernels  25.3 us (91%)
  local copies, waits for them, and re-layouts  2.26 us (8%)
    pallas_call x1, Pallas kernels, on_device_fused(): pl.pallas_call(functools.partial(fused_kernel, dims), out_shape=jax.Shape...  25.3 us
    unnamed x1, local copies, waits for them, and re-layouts  2.26 us

profile of v2, /device:TPU:0, one launch (start us, length us, event | category | flops | bytes accessed | tf_op | source)
XLA Modules:
  0.0 27.5 jit_solution(7633620167579975404)
XLA Ops:
  0.0 25.3 %shard_map.64 = bf16[2048,256]{1,0:T(8,128)(2,1)} custom-call(bf16[2048,512]{1,0:T(8,128)(2,1)} %bitcast.7, bf16[9,512,128]{2,1,0:T(8,128)(2,1)} %bitcast.8, bf16[2304,256]{1,0:T(8,128)(2,1)} %bitcast.9, f32[1,256]{1,0:T(1,128)} %bitcast.10, f32[1,256]{1,0:T(1,128)} %bitcast.11, f32[1,8]{1,0:T(1,128)} %steps_hbm.1), custom_call_target="tpu_custom_call" | custom-call | tf_op jit(solution)/shard_map/pallas_call | solution.py:382
  25.3 2.3 %copy.8 = bf16[1,8,16,16,256]{4,3,2,1,0:T(8,128)(2,1)} copy(bf16[1,8,16,16,256]{4,3,2,1,0:T(8,128)(2,1)} %bitcast.6) | data formatting | bytes 2097152

commit v3 on v2

--- a/solution.py
+++ b/solution.py
@@ -94,16 +94,17 @@
     skip_hbm,
     rates_hbm,
     steps_hbm,
-    out_hbm,
+    out_ref,
     skip_ref,
     rates_ref,
     steps_ref,
     frames_buf,
     w_in_buf,
+    w_far_buf,
     w_out_buf,
-    out_buf,
     states,
     running,
+    far_drive,
     ends,
     block_decay,
     carry,
@@ -111,9 +112,12 @@
     frame_sem,
     w_in_sem,
     w_out_sem,
-    out_sem,
-    state_send,
-    state_recv,
+    cross_send,
+    cross_recv,
+    group_send,
+    group_recv,
+    pair_send,
+    pair_recv,
     end_send,
     end_recv,
     decay_send,
@@ -126,12 +130,15 @@
     cells = height * width
     rows = group * cells
     groups_n = count // group
-    part = running.shape[1]
-    feats = out_buf.shape[1]
+    part = running.shape[2]
+    feats = out_ref.shape[1]
     chans = 2 * part
     me = lax.axis_index("chan")
     other = 1 - me
     z = lax.axis_index("tm")
+    y = lax.axis_index("groups")
+    d = lax.axis_index("dp")
+    quarter = frames_buf.shape[1] // 4
 
     def frame_copy(g):
         span = pl.ds(pl.multiple_of(g * rows, rows), rows)
@@ -145,10 +152,6 @@
         return pltpu.make_async_copy(
             w_in_hbm.at[tap], w_in_buf.at[:, place : place + part], w_in_sem.at[tap]
         )
-
-    def out_copy(g):
-        span = pl.ds(pl.multiple_of(g * rows, rows), rows)
-        return pltpu.make_async_copy(out_buf.at[span], out_hbm.at[span], out_sem.at[g])
 
     w_out_copy = pltpu.make_async_copy(w_out_hbm, w_out_buf, w_out_sem)
     small = [
@@ -166,6 +169,8 @@
 
     barrier = pltpu.get_barrier_semaphore()
     pl.semaphore_signal(barrier, inc=1, device_id={"chan": other}, device_id_type=MESH)
+    pl.semaphore_signal(barrier, inc=1, device_id={"groups": 1 - y}, device_id_type=MESH)
+    pl.semaphore_signal(barrier, inc=1, device_id={"dp": 1 - d}, device_id_type=MESH)
     for k in range(blocks):
 
         @pl.when(k != z)
@@ -176,13 +181,14 @@
         copy.wait()
     rates_all = rates_ref[...]
     rates_own = rates_ref[:, pl.ds(pl.multiple_of(me * part, part), part)]
+    rates_far = rates_ref[:, pl.ds(pl.multiple_of(other * part, part), part)]
     total = steps_ref[0, 0]
     for t in range(1, count):
         total = total + steps_ref[0, t]
     block_decay[z] = jnp.broadcast_to(jnp.exp(-rates_own * total), (8, part))
     running[...] = jnp.zeros_like(running)
     taps[...] = jnp.zeros_like(taps)
-    pl.semaphore_wait(barrier, blocks)
+    pl.semaphore_wait(barrier, blocks + 2)
 
     def decay_send_to(k):
         return pltpu.make_async_remote_copy(
@@ -206,7 +212,7 @@
 
     def end_send_to(k):
         return pltpu.make_async_remote_copy(
-            src_ref=states.at[me, count - 1],
+            src_ref=ends.at[z],
             dst_ref=ends.at[z],
             send_sem=end_send.at[k],
             recv_sem=end_recv.at[z],
@@ -216,7 +222,7 @@
 
     def end_from(k):
         return pltpu.make_async_remote_copy(
-            src_ref=states.at[me, count - 1],
+            src_ref=ends.at[k],
             dst_ref=ends.at[k],
             send_sem=end_send.at[k],
             recv_sem=end_recv.at[k],
@@ -224,15 +230,57 @@
             device_id_type=MESH,
         )
 
-    def state_copy(side, t):
-        return pltpu.make_async_remote_copy(
-            src_ref=states.at[side, t],
-            dst_ref=states.at[side, t],
-            send_sem=state_send.at[t],
-            recv_sem=state_recv.at[t],
+    def piece(buffer, row, place):
+        return buffer.at[
+            pl.ds(pl.multiple_of(row * quarter, quarter), quarter),
+            pl.ds(pl.multiple_of(place * part, part), part),
+        ]
+
+    def cross_copy(place):
+        return pltpu.make_async_remote_copy(
+            src_ref=piece(w_in_buf, 2 * y + d, place),
+            dst_ref=piece(w_far_buf, 2 * y + d, place),
+            send_sem=cross_send.at[place],
+            recv_sem=cross_recv.at[place],
             device_id={"chan": other},
             device_id_type=MESH,
         )
+
+    def group_copy(place, row):
+        return pltpu.make_async_remote_copy(
+            src_ref=piece(w_far_buf, row, place),
+            dst_ref=piece(w_far_buf, row, place),
+            send_sem=group_send.at[place],
+            recv_sem=group_recv.at[place],
+            device_id={"groups": 1 - y},
+            device_id_type=MESH,
+        )
+
+    def pair_copy(slot, place, row):
+        return pltpu.make_async_remote_copy(
+            src_ref=piece(w_far_buf, row, place),
+            dst_ref=piece(w_far_buf, row, place),
+            send_sem=pair_send.at[slot, place],
+            recv_sem=pair_recv.at[slot, place],
+            device_id={"dp": 1 - d},
+            device_id_type=MESH,
+        )
+
+    near, away = 2 * y + d, 2 * (1 - y) + d
+    near_pair, away_pair = 2 * y + 1 - d, 2 * (1 - y) + 1 - d
+
+    def pass_on(place):
+        cross_copy(place).wait_recv()
+        group_copy(place, near).start()
+        pair_copy(0, place, near).start()
+
+    def pass_pair(place):
+        group_copy(place, away).wait_recv()
+        pair_copy(1, place, away).start()
+
+    def pair_arrive(place):
+        pair_copy(0, place, near_pair).wait_recv()
+        pair_copy(1, place, away_pair).wait_recv()
 
     def carry_copy(side):
         return pltpu.make_async_remote_copy(
@@ -244,18 +292,42 @@
             device_id_type=MESH,
         )
 
+    for place in range(9):
+        w_in_copy((place % 3) * 3 + place // 3).wait()
+        cross_copy(place).start()
     for k in range(1, blocks):
 
         @pl.when(z < k)
         def _():
             decay_send_to(k).start()
 
-    for tap in range(9):
-        w_in_copy(tap).wait()
-
     column = lax.broadcasted_iota(jnp.int32, (cells, 1), 0) % width
     first_col = column == 0
     last_col = column == width - 1
+
+    def displaced_sum(mine, base):
+        zero = jnp.zeros((width, part), jnp.float32)
+        above = mine[:, base : base + part]
+        level = mine[:, base + part : base + 2 * part]
+        below = mine[:, base + 2 * part : base + 3 * part]
+        return (
+            level
+            + jnp.concatenate([zero, above[: cells - width]], axis=0)
+            + jnp.concatenate([below[width:], zero], axis=0)
+        )
+
+    def from_left(values):
+        return jnp.where(first_col, 0.0, pltpu.roll(values, 1, 0))
+
+    def from_right(values):
+        return jnp.where(last_col, 0.0, pltpu.roll(values, cells - 1, 0))
+
+    def advance(side, t, rates_part, drive):
+        decay = jnp.exp(-(rates_part * steps_ref[0, t]))
+        gain_in = (1.0 - decay) / rates_part
+        state = decay * running[side] + gain_in * drive
+        running[side] = state
+        states[side, t] = state
 
     def drive_step(g, unused):
         frame_copy(g).wait()
@@ -264,35 +336,45 @@
             frames_buf[span, :], w_in_buf[...], preferred_element_type=jnp.float32
         )
         for f in range(group):
+            mine = product[f * cells : (f + 1) * cells]
+            drive = (
+                displaced_sum(mine, 3 * part)
+                + from_left(displaced_sum(mine, 0))
+                + from_right(displaced_sum(mine, 6 * part))
+            )
+            advance(me, g * group + f, rates_own, drive)
+
+        @pl.when(g > 0)
+        def _():
+            pass_on(g - 1)
+
+        return unused
+
+    def far_step(col_off, g, unused):
+        span = pl.ds(pl.multiple_of(g * rows, rows), rows)
+        product = jnp.dot(
+            frames_buf[span, :],
+            w_far_buf[:, col_off * 3 * part : (col_off + 1) * 3 * part],
+            preferred_element_type=jnp.float32,
+        )
+        for f in range(group):
             t = g * group + f
-            mine = product[f * cells : (f + 1) * cells]
-            sums = []
-            for col_off in range(3):
-                base = col_off * 3 * part
-                above = mine[:, base : base + part]
-                level = mine[:, base + part : base + 2 * part]
-                below = mine[:, base + 2 * part : base + 3 * part]
-                zero = jnp.zeros((width, part), jnp.float32)
-                sums.append(
-                    level
-                    + jnp.concatenate([zero, above[: cells - width]], axis=0)
-                    + jnp.concatenate([below[width:], zero], axis=0)
-                )
-            drive = (
-                sums[1]
-                + jnp.where(first_col, 0.0, pltpu.roll(sums[0], 1, 0))
-                + jnp.where(last_col, 0.0, pltpu.roll(sums[2], cells - 1, 0))
-            )
-            scaled = rates_own * steps_ref[0, t]
-            decay = jnp.exp(-scaled)
-            gain_in = (1.0 - decay) / rates_own
-            state = decay * running[...] + gain_in * drive
-            running[...] = state
-            states[me, t] = state.astype(jnp.bfloat16)
-            state_copy(me, t).start()
+            sums = displaced_sum(product[f * cells : (f + 1) * cells], 0)
+            if col_off == 0:
+                far_drive[t] = from_left(sums)
+            elif col_off == 1:
+                far_drive[t] = far_drive[t] + sums
+            else:
+                advance(other, t, rates_far, far_drive[t] + from_right(sums))
         return unused
 
+    def far_part(col_off):
+        for place in range(3 * col_off, 3 * col_off + 3):
+            pair_arrive(place)
+        lax.fori_loop(0, groups_n, functools.partial(far_step, col_off), 0)
+
     lax.fori_loop(0, groups_n, drive_step, 0)
+    ends[z] = running[me].astype(jnp.bfloat16)
 
     for k in reversed(range(1, blocks)):
 
@@ -300,17 +382,33 @@
         def _():
             end_send_to(k).start()
 
-    running[...] = jnp.zeros_like(running)
+    passed = groups_n - 1
+    for place in range(passed, 5):
+        pass_on(place)
+    for place in range(3):
+        pass_pair(place)
+    far_part(0)
+    for place in range(5, 8):
+        pass_on(place)
+    for place in range(3, 6):
+        pass_pair(place)
+    pass_on(8)
+    far_part(1)
+
+    running[me] = jnp.zeros_like(running[me])
     for k in range(blocks - 1):
 
         @pl.when(k < z)
         def _():
             decay_from(k).wait_recv()
             end_from(k).wait_recv()
-            running[...] = block_decay[k][:1] * running[...] + ends[k].astype(jnp.float32)
-
-    carry[me] = running[...].astype(jnp.bfloat16)
+            running[me] = block_decay[k][:1] * running[me] + ends[k].astype(jnp.float32)
+
+    carry[me] = running[me].astype(jnp.bfloat16)
     carry_copy(me).start()
+    for place in range(6, 9):
+        pass_pair(place)
+    far_part(2)
     w_out_copy.wait()
     carry_copy(other).wait_recv()
 
@@ -320,12 +418,11 @@
         span = pl.ds(pl.multiple_of(g * rows, rows), rows)
         for f in range(group):
             t = g * group + f
-            state_copy(other, t).wait_recv()
             elapsed = elapsed + steps_ref[0, t]
             product = jnp.exp(-rates_all * elapsed)
             for side in range(2):
                 lanes = slice(side * part, (side + 1) * part)
-                state = states[side, t].astype(jnp.float32) + product[:, lanes] * carry[
+                state = states[side, t] + product[:, lanes] * carry[
                     side
                 ].astype(jnp.float32)
                 state = state.astype(jnp.bfloat16).astype(jnp.float32)
@@ -349,16 +446,16 @@
             )
             result = term if result is None else result + term
         result = result + skip_ref[...] * frames_buf[span, own_feats].astype(jnp.float32)
-        out_buf[span, :] = result.astype(jnp.bfloat16)
-        out_copy(g).start()
+        out_ref[span, :] = result.astype(jnp.bfloat16)
         return elapsed
 
     lax.fori_loop(0, groups_n, mix_step, jnp.float32(0.0))
 
-    for g in range(groups_n):
-        out_copy(g).wait()
-    for t in range(count):
-        state_copy(me, t).wait_send()
+    for place in range(9):
+        cross_copy(place).wait_send()
+        group_copy(place, near).wait_send()
+        pair_copy(0, place, near).wait_send()
+        pair_copy(1, place, away).wait_send()
     carry_copy(me).wait_send()
     for k in range(1, blocks):
 
@@ -383,17 +480,18 @@
         functools.partial(fused_kernel, dims),
         out_shape=jax.ShapeDtypeStruct((count * cells, feats), jnp.bfloat16),
         in_specs=[hbm] * 6,
-        out_specs=pl.BlockSpec(memory_space=pl.ANY),
+        out_specs=pl.BlockSpec(memory_space=pltpu.VMEM),
         scratch_shapes=[
             pltpu.VMEM((1, feats), jnp.float32),
             pltpu.VMEM((1, chans), jnp.float32),
             pltpu.SMEM((1, count), jnp.float32),
             pltpu.VMEM((count * cells, feats_in), jnp.bfloat16),
             pltpu.VMEM((feats_in, 9 * part), jnp.bfloat16),
+            pltpu.VMEM((feats_in, 9 * part), jnp.bfloat16),
             pltpu.VMEM((9 * chans, feats), jnp.bfloat16),
-            pltpu.VMEM((count * cells, feats), jnp.bfloat16),
-            pltpu.VMEM((2, count, cells, part), jnp.bfloat16),
-            pltpu.VMEM((cells, part), jnp.float32),
+            pltpu.VMEM((2, count, cells, part), jnp.float32),
+            pltpu.VMEM((2, cells, part), jnp.float32),
+            pltpu.VMEM((count, cells, part), jnp.float32),
             pltpu.VMEM((blocks, cells, part), jnp.bfloat16),
             pltpu.VMEM((blocks, 8, part), jnp.float32),
             pltpu.VMEM((2, cells, part), jnp.bfloat16),
@@ -401,9 +499,12 @@
             dma((groups_n,)),
             dma((9,)),
             dma,
-            dma((groups_n,)),
-            dma((count,)),
-            dma((count,)),
+            dma((9,)),
+            dma((9,)),
+            dma((9,)),
+            dma((9,)),
+            dma((2, 9)),
+            dma((2, 9)),
             dma((blocks,)),
             dma((blocks,)),
             dma((blocks,)),
@@ -430,8 +531,10 @@
     clips, count, height, width = frames.shape[:4]
     fused = (
         mesh.shape["chan"] == 2
+        and mesh.shape["groups"] == 2
+        and mesh.shape["dp"] == 2
         and clips == 1
-        and count % 2 == 0
+        and count == 8
         and width == 16
         and w_in.shape[3] == LANES
         and w_out.shape[3] % LANES == 0

time: 27.7 us -> 32.2 us (1.16)
  Pallas kernels: 25.3 us -> 29.8 us
    pallas_call x1, Pallas kernels: 25.3 us -> 29.8 us  [on_device_fused(): pl.pallas_call(functools.partial(fused_kernel, dims), out_shape=jax.Shape...]
where the time goes in v3:
time: 32.2 us; the launch traced here: 32 us
  Pallas kernels  29.8 us (93%)
  local copies, waits for them, and re-layouts  2.26 us (7%)
    pallas_call x1, Pallas kernels, on_device_fused(): pl.pallas_call(functools.partial(fused_kernel, dims), out_shape=jax.Shape...  29.8 us
    unnamed x1, local copies, waits for them, and re-layouts  2.26 us

profile of v3, /device:TPU:0, one launch (start us, length us, event | category | flops | bytes accessed | tf_op | source)
XLA Modules:
  0.0 32.0 jit_solution(14878521094261447014)
XLA Ops:
  0.0 29.8 %shard_map.64 = bf16[2048,256]{1,0:T(8,128)(2,1)} custom-call(bf16[2048,512]{1,0:T(8,128)(2,1)} %bitcast.7, bf16[9,512,128]{2,1,0:T(8,128)(2,1)} %bitcast.8, bf16[2304,256]{1,0:T(8,128)(2,1)} %bitcast.9, f32[1,256]{1,0:T(1,128)} %bitcast.10, f32[1,256]{1,0:T(1,128)} %bitcast.11, f32[1,8]{1,0:T(1,128)} %steps_hbm.1), custom_call_target="tpu_custom_call" | custom-call | tf_op jit(solution)/shard_map/pallas_call | solution.py:479
  29.8 2.3 %copy.8 = bf16[1,8,16,16,256]{4,3,2,1,0:T(8,128)(2,1)} copy(bf16[1,8,16,16,256]{4,3,2,1,0:T(8,128)(2,1)} %bitcast.6) | data formatting | bytes 2097152

commit v4 on v2

--- a/solution.py
+++ b/solution.py
@@ -126,6 +126,7 @@
     cells = height * width
     rows = group * cells
     groups_n = count // group
+    early = (5 * count) // 8
     part = running.shape[1]
     feats = out_buf.shape[1]
     chans = 2 * part
@@ -289,7 +290,11 @@
             state = decay * running[...] + gain_in * drive
             running[...] = state
             states[me, t] = state.astype(jnp.bfloat16)
-            state_copy(me, t).start()
+
+            @pl.when(t < early)
+            def _():
+                state_copy(me, t).start()
+
         return unused
 
     lax.fori_loop(0, groups_n, drive_step, 0)
@@ -311,6 +316,8 @@
 
     carry[me] = running[...].astype(jnp.bfloat16)
     carry_copy(me).start()
+    for t in range(early, count):
+        state_copy(me, t).start()
     w_out_copy.wait()
     carry_copy(other).wait_recv()
 

time: 27.7 us -> 24.9 us (0.90)
  Pallas kernels: 25.3 us -> 22.4 us
    pallas_call x1, Pallas kernels: 25.3 us -> 22.4 us  [on_device_fused(): pl.pallas_call(functools.partial(fused_kernel, dims), out_shape=jax.Shape...]
where the time goes in v4:
time: 24.9 us; the launch traced here: 24.7 us
  Pallas kernels  22.4 us (90%)
  local copies, waits for them, and re-layouts  2.26 us (9%)
    pallas_call x1, Pallas kernels, on_device_fused(): pl.pallas_call(functools.partial(fused_kernel, dims), out_shape=jax.Shape...  22.4 us
    unnamed x1, local copies, waits for them, and re-layouts  2.26 us

profile of v4, /device:TPU:0, one launch (start us, length us, event | category | flops | bytes accessed | tf_op | source)
XLA Modules:
  0.0 24.7 jit_solution(140027488721811683)
XLA Ops:
  0.0 22.4 %shard_map.64 = bf16[2048,256]{1,0:T(8,128)(2,1)} custom-call(bf16[2048,512]{1,0:T(8,128)(2,1)} %bitcast.7, bf16[9,512,128]{2,1,0:T(8,128)(2,1)} %bitcast.8, bf16[2304,256]{1,0:T(8,128)(2,1)} %bitcast.9, f32[1,256]{1,0:T(1,128)} %bitcast.10, f32[1,256]{1,0:T(1,128)} %bitcast.11, f32[1,8]{1,0:T(1,128)} %steps_hbm.1), custom_call_target="tpu_custom_call" | custom-call | tf_op jit(solution)/shard_map/pallas_call | solution.py:389
  22.4 2.3 %copy.8 = bf16[1,8,16,16,256]{4,3,2,1,0:T(8,128)(2,1)} copy(bf16[1,8,16,16,256]{4,3,2,1,0:T(8,128)(2,1)} %bitcast.6) | data formatting | bytes 2097152

commit v5 on v4

--- a/solution.py
+++ b/solution.py
@@ -94,14 +94,13 @@
     skip_hbm,
     rates_hbm,
     steps_hbm,
-    out_hbm,
+    out_ref,
     skip_ref,
     rates_ref,
     steps_ref,
     frames_buf,
     w_in_buf,
     w_out_buf,
-    out_buf,
     states,
     running,
     ends,
@@ -111,7 +110,6 @@
     frame_sem,
     w_in_sem,
     w_out_sem,
-    out_sem,
     state_send,
     state_recv,
     end_send,
@@ -128,7 +126,7 @@
     groups_n = count // group
     early = (5 * count) // 8
     part = running.shape[1]
-    feats = out_buf.shape[1]
+    feats = out_ref.shape[1]
     chans = 2 * part
     me = lax.axis_index("chan")
     other = 1 - me
@@ -146,10 +144,6 @@
         return pltpu.make_async_copy(
             w_in_hbm.at[tap], w_in_buf.at[:, place : place + part], w_in_sem.at[tap]
         )
-
-    def out_copy(g):
-        span = pl.ds(pl.multiple_of(g * rows, rows), rows)
-        return pltpu.make_async_copy(out_buf.at[span], out_hbm.at[span], out_sem.at[g])
 
     w_out_copy = pltpu.make_async_copy(w_out_hbm, w_out_buf, w_out_sem)
     small = [
@@ -356,14 +350,11 @@
             )
             result = term if result is None else result + term
         result = result + skip_ref[...] * frames_buf[span, own_feats].astype(jnp.float32)
-        out_buf[span, :] = result.astype(jnp.bfloat16)
-        out_copy(g).start()
+        out_ref[span, :] = result.astype(jnp.bfloat16)
         return elapsed
 
     lax.fori_loop(0, groups_n, mix_step, jnp.float32(0.0))
 
-    for g in range(groups_n):
-        out_copy(g).wait()
     for t in range(count):
         state_copy(me, t).wait_send()
     carry_copy(me).wait_send()
@@ -390,7 +381,7 @@
         functools.partial(fused_kernel, dims),
         out_shape=jax.ShapeDtypeStruct((count * cells, feats), jnp.bfloat16),
         in_specs=[hbm] * 6,
-        out_specs=pl.BlockSpec(memory_space=pl.ANY),
+        out_specs=pl.BlockSpec(memory_space=pltpu.VMEM),
         scratch_shapes=[
             pltpu.VMEM((1, feats), jnp.float32),
             pltpu.VMEM((1, chans), jnp.float32),
@@ -398,7 +389,6 @@
             pltpu.VMEM((count * cells, feats_in), jnp.bfloat16),
             pltpu.VMEM((feats_in, 9 * part), jnp.bfloat16),
             pltpu.VMEM((9 * chans, feats), jnp.bfloat16),
-            pltpu.VMEM((count * cells, feats), jnp.bfloat16),
             pltpu.VMEM((2, count, cells, part), jnp.bfloat16),
             pltpu.VMEM((cells, part), jnp.float32),
             pltpu.VMEM((blocks, cells, part), jnp.bfloat16),
@@ -408,7 +398,6 @@
             dma((groups_n,)),
             dma((9,)),
             dma,
-            dma((groups_n,)),
             dma((count,)),
             dma((count,)),
             dma((blocks,)),
@@ -420,15 +409,20 @@
             dma((3,)),
         ],
         compiler_params=pltpu.CompilerParams(
-            collective_id=0, has_side_effects=True, vmem_limit_bytes=62 << 20
+            collective_id=0, has_side_effects=True, vmem_limit_bytes=48 << 20
         ),
     )(
-        frames.reshape(count * cells, feats_in),
-        w_in.reshape(9, feats_in, part),
-        w_out.reshape(9 * chans, feats),
-        skip.reshape(1, feats),
-        rates.reshape(1, chans),
-        steps_dt,
+        *[
+            pltpu.with_memory_space_constraint(array, pltpu.HBM)
+            for array in (
+                frames.reshape(count * cells, feats_in),
+                w_in.reshape(9, feats_in, part),
+                w_out.reshape(9 * chans, feats),
+                skip.reshape(1, feats),
+                rates.reshape(1, chans),
+                steps_dt,
+            )
+        ]
     )
     return out.reshape(1, count, height, width, feats)
 

time: 24.9 us -> 22.8 us (0.916)
  local copies, waits for them, and re-layouts: 2.26 us -> 0.97 us
  Pallas kernels: 22.4 us -> 21.7 us
    unnamed x1, local copies, waits for them, and re-layouts: 2.26 us -> 0.97 us
    pallas_call x1, Pallas kernels: 22.4 us -> 21.7 us  [on_device_fused(): pl.pallas_call(functools.partial(fused_kernel, dims), out_shape=jax.Shape...]
where the time goes in v5:
time: 22.8 us; the launch traced here: 22.7 us
  Pallas kernels  21.7 us (95%)
  local copies, waits for them, and re-layouts  0.97 us (4%)
    pallas_call x1, Pallas kernels, on_device_fused(): pl.pallas_call(functools.partial(fused_kernel, dims), out_shape=jax.Shape...  21.7 us
    unnamed x1, local copies, waits for them, and re-layouts  0.97 us

profile of v5, /device:TPU:0, one launch (start us, length us, event | category | flops | bytes accessed | tf_op | source)
XLA Modules:
  0.0 22.7 jit_solution(1927836892870407687)
XLA Ops:
  0.0 21.7 %shard_map.64 = bf16[2048,256]{1,0:T(8,128)(2,1)S(1)} custom-call(bf16[2048,512]{1,0:T(8,128)(2,1)} %bitcast.7, bf16[9,512,128]{2,1,0:T(8,128)(2,1)} %bitcast.8, bf16[2304,256]{1,0:T(8,128)(2,1)} %bitcast.9, f32[1,256]{1,0:T(1,128)} %bitcast.10, f32[1,256]{1,0:T(1,128)} %bitcast.11, f32[1,8]{1,0:T(1,128)} %steps_hbm.1), custom_call_target="tpu_custom_call" | custom-call | tf_op jit(solution)/shard_map/pallas_call | solution.py:380
  21.7 1.0 %copy.8 = bf16[1,8,16,16,256]{4,3,2,1,0:T(8,128)(2,1)} copy(bf16[1,8,16,16,256]{4,3,2,1,0:T(8,128)(2,1)S(1)} %bitcast.6) | data formatting | bytes 2097152
